TPU v7x, 128 devices: a whole 4x4x4 slice. The times are simulated.
128 devices in a mesh: grp: 16 (over y, x), voc: 8 (over z, core).
Axes of the slice: x: 4, y: 4, z: 4, core: 2. Of those that a mesh axis runs over, the one named last changes fastest.
Arguments:
- teacher_rows: bfloat16 [512, 4096], P(('grp', 'voc')), may hold values from -125 to 125
- student_rows: bfloat16 [512, 4096], P(('grp', 'voc')), may hold values from -125 to 125
- teacher_head: bfloat16 [4096, 98304], P(None, ('grp', 'voc')), may hold values from -4 to 4
- student_head: bfloat16 [4096, 98304], P(None, ('grp', 'voc')), may hold values from -4 to 4
- response_ids: int32 [512], replicated, may hold values from 0 to 98303
- lengths: int32 [4], replicated, may hold values from 1 to 128, 384 in all
- seq_order: int32 [4], replicated, may hold values from 0 to 3, each once
Outputs:
- token_kl: float32 [512], P(('grp', 'voc'))
- sampled_gap: float32 [512], P(('grp', 'voc'))
- head_grad: bfloat16 [4096, 98304], P(None, ('grp', 'voc'))
- hidden_grad: bfloat16 [512, 4096], P(('grp', 'voc'))
Inputs may be any that keep to these rules, and one draw needn't show every extreme that they name: The lengths sum to exactly 384.
All inputs are finite; a program needn't handle non-finite values.
Results may differ from a plain program's by a relative error of at most 0.017.
Values may be sent and summed in bfloat16 or wider, within the bound.
No kernel may reach another device: no remote copies, remote signals or barrier semaphores. Data moves between devices by JAX's collectives and lax.ppermute only.
A program may use at most 128 MiB of HBM per device.

v0:
```python
import jax
import jax.numpy as jnp
from jax import lax
from jax.sharding import PartitionSpec as P

loss_scale = 64.0


def body(teacher_rows, student_rows, teacher_head, student_head, response_ids, lengths, seq_order):
    own_rows = student_rows.shape[0]
    depth = student_rows.shape[1]
    width = student_head.shape[1]
    place = lax.axis_index(("grp", "voc"))
    first = place * width
    seq_count = lengths.shape[0]
    total = response_ids.shape[0]
    span = total // seq_count
    teacher_all, student_all = (
        lax.all_gather(teacher_rows, ("grp", "voc"), axis=0, tiled=True),
        lax.all_gather(student_rows, ("grp", "voc"), axis=0, tiled=True),
    )
    teacher_all = teacher_all.reshape(seq_count, span, depth)[seq_order].reshape(total, depth)
    live = (jnp.arange(span, dtype=jnp.int32)[None, :] < lengths[:, None]).reshape(total)
    weight = live.astype(jnp.float32)
    student_logits = jnp.dot(student_all, student_head, preferred_element_type=jnp.float32)
    teacher_logits = jnp.dot(teacher_all, teacher_head, preferred_element_type=jnp.float32)
    spread = student_logits - teacher_logits
    column = first + jnp.arange(width, dtype=jnp.int32)
    hit = jnp.sum(jnp.where(response_ids[:, None] == column[None, :], spread, 0.0), axis=1)
    top_s, top_t = lax.pmax(
        (jnp.max(student_logits, axis=1), jnp.max(teacher_logits, axis=1)), ("grp", "voc")
    )
    scaled = jnp.exp(student_logits - top_s[:, None])
    sum_s, moment, sum_t, hit = lax.psum(
        (
            jnp.sum(scaled, axis=1),
            jnp.sum(scaled * spread, axis=1),
            jnp.sum(jnp.exp(teacher_logits - top_t[:, None]), axis=1),
            hit,
        ),
        ("grp", "voc"),
    )
    student_lse = top_s + jnp.log(sum_s)
    teacher_lse = top_t + jnp.log(sum_t)
    average = moment / sum_s
    kl_rows = weight * (average - student_lse + teacher_lse)
    gap_rows = weight * (hit - student_lse + teacher_lse)
    logit_grad = (
        (loss_scale * weight)[:, None]
        * jnp.exp(student_logits - student_lse[:, None])
        * (spread - average[:, None])
    ).astype(jnp.bfloat16)
    head_grad = lax.dot_general(
        student_all, logit_grad, (((0,), (0,)), ((), ())), preferred_element_type=jnp.float32
    ).astype(jnp.bfloat16)
    hidden_grad = lax.psum_scatter(
        lax.dot_general(
            logit_grad, student_head, (((1,), (1,)), ((), ())), preferred_element_type=jnp.float32
        ),
        ("grp", "voc"),
        scatter_dimension=0,
        tiled=True,
    ).astype(jnp.bfloat16)
    token_kl = lax.dynamic_slice_in_dim(kl_rows, place * own_rows, own_rows)
    sampled_gap = lax.dynamic_slice_in_dim(gap_rows, place * own_rows, own_rows)
    return (token_kl, sampled_gap, head_grad, hidden_grad)


def solution(mesh):
    in_specs = (
        P(("grp", "voc"), None),
        P(("grp", "voc"), None),
        P(None, ("grp", "voc")),
        P(None, ("grp", "voc")),
        P(),
        P(),
        P(),
    )
    out_specs = (
        P(("grp", "voc")),
        P(("grp", "voc")),
        P(None, ("grp", "voc")),
        P(("grp", "voc"), None),
    )
    return jax.shard_map(body, mesh=mesh, in_specs=in_specs, out_specs=out_specs, check_vma=False)
```

profile of v0, /device:TPU:1, one launch (start us, length us, event | category | flops | bytes accessed | tf_op | source)
XLA Modules:
  0.0 440.2 jit_solution(2345942377943160696)
XLA Ops:
  7.2 0.7 all-gather.5.cloned.1.call-update
  7.9 0.0 all-gather.7.cloned.1.call-start
  7.9 0.7 all-gather.7.cloned.1.call-update
  8.7 0.7 compare_select_fusion
  9.3 0.7 fusion.3
  10.1 71.7 %all-gather.5.cloned.1.call-done = bf16[128,4,4096]{2,1,0:T(4,128)(2,1)} async-done(((bf16[1,4,4096]{2,1,0:T(4,128)(2,1)}), bf16[128,4,4096]{2,1,0:T(4,128)(2,1)}) %all-gather.5.cloned.1.call-update) | async-done | bytes 4194320 | tf_op jit(solution)/shard_map/all_gather | solution.py:20
  81.7 6.9 %reshape.50 = bf16[512,4096]{1,0:T(8,128)(2,1)} reshape(bf16[128,4,4096]{2,1,0:T(4,128)(2,1)} %all-gather.5.cloned.1.call-done) | data formatting | bytes 8388608
  88.6 7.2 %fusion.4 = (f32[512]{0:T(512)S(1)}, f32[512,768]{1,0:T(8,128)S(1)}) fusion(bf16[512,4096]{1,0:T(8,128)(2,1)} %reshape.50, bf16[4096,768]{1,0:T(8,128)(2,1)} %param.10), kind=kOutput, calls=%fused_computation.20 | convolution fusion | flops 3221618176 | bytes 12060672 | tf_op jit(solution)/shard_map/dot_general | solution.py:25
  95.8 53.5 %all-gather.7.cloned.1.call-done = bf16[128,4,4096]{2,1,0:T(4,128)(2,1)} async-done(((bf16[1,4,4096]{2,1,0:T(4,128)(2,1)}), bf16[128,4,4096]{2,1,0:T(4,128)(2,1)}) %all-gather.7.cloned.1.call-update) | async-done | bytes 4194320 | tf_op jit(solution)/shard_map/all_gather | solution.py:19
  149.3 6.9 %reshape.38 = bf16[4,128,4096]{2,1,0:T(8,128)(2,1)} reshape(bf16[128,4,4096]{2,1,0:T(4,128)(2,1)} %all-gather.7.cloned.1.call-done) | data formatting | bytes 8388608 | tf_op jit(solution)/shard_map/reshape | solution.py:22
  156.2 4.9 %gather_fusion = bf16[4,128,4096]{2,1,0:T(8,128)(2,1)} fusion(bf16[4,128,4096]{2,1,0:T(8,128)(2,1)} %reshape.38, s32[1024]{0:T(1024)S(1)} %pad_clamp_fusion), kind=kCustom, calls=%fused_computation | custom fusion | bytes 8388624 | tf_op jit(solution)/shard_map/gather | solution.py:22
  161.1 8.7 %fusion.5 = (f32[512]{0:T(512)S(1)}, f32[512,768]{1,0:T(8,128)}) fusion(bf16[512,4096]{1,0:T(8,128)(2,1)} %bitcast.21, bf16[4096,768]{1,0:T(8,128)(2,1)} %param.9), kind=kOutput, calls=%fused_computation.21 | convolution fusion | flops 3221618176 | bytes 12060672 | tf_op jit(solution)/shard_map/dot_general | solution.py:26
  169.8 62.4 %all-reduce.3 = (f32[512]{0:T(512)S(1)}, f32[512]{0:T(512)S(1)}) all-reduce(f32[512]{0:T(512)S(1)} %get-tuple-element.28, f32[512]{0:T(512)S(1)} %get-tuple-element.30), channel_id=1, replica_groups=mesh['grp'=16,'voc'=8] {'grp','voc'}, use_global_device_ids=true, to_apply=%region_1.2 | all-reduce | flops 1024 | bytes 8192 | tf_op jit(solution)/shard_map/pmax | solution.py:30
  232.2 2.6 fusion.1
  234.7 64.2 %all-reduce.2 = (f32[512]{0:T(512)S(1)}, f32[512]{0:T(512)S(1)}) all-reduce(f32[512]{0:T(512)S(1)} %get-tuple-element.13, f32[512]{0:T(512)S(1)} %get-tuple-element.12), channel_id=1, replica_groups=mesh['grp'=16,'voc'=8] {'grp','voc'}, use_global_device_ids=true, to_apply=%region_3.4 | all-reduce | flops 1024 | bytes 8192 | tf_op jit(solution)/shard_map/psum | solution.py:34
  298.9 0.4 multiply_convert_fusion
  299.4 8.6 %fusion.6 = f32[512,4096]{1,0:T(8,128)} fusion(bf16[512,768]{1,0:T(8,128)(2,1)S(1)} %multiply_convert_fusion, bf16[4096,768]{1,0:T(8,128)(2,1)} %param.10), kind=kOutput, calls=%fused_computation.22 | convolution fusion | flops 3221225472 | bytes 15466496 | tf_op jit(solution)/shard_map/dot_general | solution.py:57
  308.0 5.3 %fusion = bf16[4096,768]{0,1:T(8,128)(2,1)} fusion(bf16[512,768]{1,0:T(8,128)(2,1)S(1)} %multiply_convert_fusion, bf16[512,4096]{1,0:T(8,128)(2,1)S(1)} %copy-done), kind=kOutput, calls=%fused_computation.2 | convolution fusion | flops 3224371200 | bytes 11272192 | tf_op jit(solution)/shard_map/dot_general | solution.py:53
  313.4 108.7 %all-reduce.5 = (f32[512]{0:T(512)S(1)}, f32[512]{0:T(512)S(1)}, bf16[512,4096]{1,0:T(8,128)(2,1)}) all-reduce(f32[512]{0:T(512)S(1)} %get-tuple-element.23, f32[512]{0:T(512)S(1)} %get-tuple-element.14, f32[512,4096]{1,0:T(8,128)} %fusion.6), channel_id=1, replica_groups=mesh['grp'=16,'voc'=8] {'grp','voc'}, use_global_device_ids=true, to_apply=%region_9.10 | all-reduce | flops 2098176 | bytes 12591104 | tf_op jit(solution)/shard_map/psum | solution.py:34
  422.1 0.1 add_select_fusion
  422.1 0.6 dynamic_slice.7
  422.7 0.6 dynamic_slice.6
  423.3 8.6 %copy.12 = bf16[4096,768]{1,0:T(8,128)(2,1)} copy(bf16[4096,768]{0,1:T(8,128)(2,1)} %fusion) | data formatting | bytes 12582912
  431.9 1.5 dynamic-slice_convert_fusion
  (10 shorter events, 0.1 us)
Async XLA Ops:
  7.2 74.6 %all-gather.5.cloned.1.call-start = ((), (), s32[]{:S(2)}) async-start(), calls=%async_computation | async-start | bytes 4227072 | tf_op jit(solution)/shard_map/all_gather | solution.py:20
  7.9 141.4 %all-gather.7.cloned.1.call-start = ((), (), s32[]{:S(2)}) async-start(), calls=%async_computation.1 | async-start | bytes 4227072 | tf_op jit(solution)/shard_map/all_gather | solution.py:19
  161.1 71.0 %copy-start.1 = (s32[512]{0:T(512)S(1)}, s32[512]{0:T(512)}, u32[]{:S(2)}) copy-start(s32[512]{0:T(512)} %param.11) | copy-start | bytes 6148
  299.4 8.7 %copy-start = (bf16[512,4096]{1,0:T(8,128)(2,1)S(1)}, bf16[512,4096]{1,0:T(8,128)(2,1)}, u32[]{:S(2)}) copy-start(bf16[512,4096]{1,0:T(8,128)(2,1)} %reshape.50) | copy-start | bytes 12582916
  313.4 108.7 %copy-start.2 = (s32[4]{0:T(128)S(1)}, s32[4]{0:T(128)}, u32[]{:S(2)}) copy-start(s32[4]{0:T(128)} %param.12) | copy-start | bytes 52
Sparse Core Ops, SparseCore 0:
  11.2 70.5 all-gather.4
  84.9 64.3 all-gather.6
where the time goes:
time: 443 us; the launch traced here: 440 us
  blocking collectives  235 us (53%)
  waiting for transfers between devices  127 us (29%)
  local copies, waits for them, and re-layouts  30 us (7%)
  matrix products  29.8 us (7%)
  between operations  14.1 us (3%)
  other arithmetic  4.43 us (1%)
    psum x2, blocking collectives, body(): lax.psum((jnp.sum(scaled, axis=1), jnp.sum(scaled * spread, axis=1), jnp....  173 us
    all_gather x1, waiting for transfers between devices, body(): lax.all_gather(student_rows, ('grp', 'voc'), axis=0, tiled=True)  71.7 us
    pmax x1, blocking collectives, body(): lax.pmax((jnp.max(student_logits, axis=1), jnp.max(teacher_logits, axis=1...  62.4 us
    all_gather x1, waiting for transfers between devices, body(): lax.all_gather(teacher_rows, ('grp', 'voc'), axis=0, tiled=True)  53.5 us
    unnamed x8, local copies, waits for them, and re-layouts  15.5 us
  transfers between devices with their start and end apart: 2, of which 2 were waited for; matrix products, arithmetic and copies ran while one was open for 4% of the time, Pallas kernels for 0%

commit v1 on v0

v1 whole, which is shorter than its diff:
```python
import jax
import jax.numpy as jnp
from jax import lax
from jax.experimental import pallas as pl
from jax.experimental.pallas import tpu as pltpu
from jax.sharding import PartitionSpec as P

AXES = ("grp", "voc")
LOSS_SCALE = 64.0
SIDE = 4
CHIPS = SIDE**3
VMEM_LIMIT = 56 * 1024 * 1024
f32 = jnp.float32
bf16 = jnp.bfloat16


def at(y, x, z, c):
    return ((y * SIDE + x) * SIDE + z) * 2 + c


RANGE = range(SIDE)
PLANES = [[at(y, x, z, 0) for x in RANGE for z in RANGE] for y in RANGE] + [
    [at(y, x, z, 1) for y in RANGE for z in RANGE] for x in RANGE
]
CORES = [[2 * chip + c for chip in range(CHIPS)] for c in range(2)]
SWAP = [(i, i ^ 1) for i in range(2 * CHIPS)]
STEPS = (0, 1, 3, 2)


def along(step):
    pairs = []
    for y in RANGE:
        for x in RANGE:
            for z in RANGE:
                pairs.append((at(y, x, z, 0), at((y - step) % SIDE, x, z, 0)))
                pairs.append((at(y, x, z, 1), at(y, (x - step) % SIDE, z, 1)))
    return pairs


def swap(value):
    return lax.ppermute(value, AXES, SWAP)


def gather_chips(shard):
    wide = jnp.broadcast_to(shard[None], (SIDE * SIDE,) + shard.shape).reshape(-1, shard.shape[1])
    plane = lax.all_to_all(wide, AXES, 0, 0, axis_index_groups=PLANES, tiled=True)
    own = [plane] + [lax.ppermute(plane, AXES, along(step)) for step in STEPS[1:]]
    return own + [swap(piece) for piece in own]


def load_rows(meta, pieces, rows, sems):
    y, x, c = meta[0], meta[1], meta[2]
    half = pieces[0].shape[1]
    copies = []
    for index, piece in enumerate(pieces):
        step = STEPS[index % SIDE]
        kind = c if index < SIDE else 1 - c
        for p in range(SIDE):
            row = jnp.where(kind == 0, (y + step) % SIDE, p)
            col = jnp.where(kind == 0, p, (x + step) % SIDE)
            row = meta[4 + row]
            start = pl.multiple_of((row * SIDE + col) * 32, 32)
            lane = pl.multiple_of(kind * half, half)
            copies.append(
                pltpu.make_async_copy(
                    piece.at[pl.ds(32 * p, 32), :],
                    rows.at[pl.ds(start, 32), pl.ds(lane, half)],
                    sems.at[index * SIDE + p],
                )
            )
    for copy in copies:
        copy.start()
    for copy in copies:
        copy.wait()


def student_kernel(meta, *refs):
    pieces, (head, logits, rows, sems) = refs[:8], refs[8:]

    @pl.when(pl.program_id(0) == 0)
    def _():
        load_rows(meta, pieces, rows, sems)

    logits[...] = jnp.dot(rows[...], head[...], preferred_element_type=f32)


def teacher_kernel(meta, *refs):
    pieces, (head, student, ids, scaled, spread, stats, rows, teacher, table, sems) = refs[:8], refs[8:]
    n = pl.program_id(0)
    total, width = student.shape
    tile = head.shape[1]

    @pl.when(n == 0)
    def _():
        load_rows(meta, pieces, rows, sems)

    teacher[:, pl.ds(pl.multiple_of(n * tile, tile), tile)] = jnp.dot(
        rows[...], head[...], preferred_element_type=f32
    )

    @pl.when(n == pl.num_programs(0) - 1)
    def _():
        chunk = 64
        first = meta[3]

        @pl.loop(0, total // chunk)
        def _(i):
            here = pl.ds(pl.multiple_of(i * chunk, chunk), chunk)
            s, t = student[here, :], teacher[here, :]
            gap = s - t
            top_s = jnp.max(s, axis=1, keepdims=True)
            top_t = jnp.max(t, axis=1, keepdims=True)
            e = jnp.exp(s - top_s)
            column = first + lax.broadcasted_iota(jnp.int32, (chunk, width), 1)
            values = (
                top_s,
                jnp.sum(e, axis=1, keepdims=True),
                jnp.sum(e * gap, axis=1, keepdims=True),
                top_t,
                jnp.sum(jnp.exp(t - top_t), axis=1, keepdims=True),
                jnp.sum(jnp.where(column == ids[here, :], gap, 0.0), axis=1, keepdims=True),
            )
            scaled[here, :] = e
            spread[here, :] = gap
            lane = lax.broadcasted_iota(jnp.int32, (chunk, 128), 1)
            packed = jnp.zeros((chunk, 128), f32)
            for k, value in enumerate(values):
                packed = jnp.where(lane == k, value, packed)
            table[here, :] = packed

        stats[...] = table[...].T[:8]


def grad_kernel(meta, scaled, spread, stats, gathered, head, grad, hidden):
    total = scaled.shape[0]

    @pl.when(pl.program_id(0) == 0)
    def _():
        tops = gathered[:, 0:total]
        top = jnp.max(tops, axis=0, keepdims=True)
        factor = jnp.exp(tops - top)
        sums = jnp.sum(gathered[:, total : 2 * total] * factor, axis=0, keepdims=True)
        moment = jnp.sum(gathered[:, 2 * total : 3 * total] * factor, axis=0, keepdims=True)
        lse = top + jnp.log(sums)
        token = lax.broadcasted_iota(jnp.int32, (1, total), 1)
        live = jnp.zeros((1, total), f32)
        span = total // 4
        for k in range(4):
            inside = (token >= k * span) & (token < k * span + meta[8 + k])
            live = jnp.where(inside, LOSS_SCALE, live)
        weight = live * jnp.exp(stats[0:1, :] - lse)
        average = moment / sums
        line = lax.broadcasted_iota(jnp.int32, (128, total), 0)
        columns = jnp.where(line == 0, weight, jnp.where(line == 1, average, 0.0)).T
        grad[...] = (columns[:, 0:1] * scaled[...] * (spread[...] - columns[:, 1:2])).astype(bf16)

    hidden[...] = lax.dot_general(
        grad[...], head[...], (((1,), (1,)), ((), ())), preferred_element_type=f32
    ).astype(hidden.dtype)


def hidden_kernel(meta, grad, head, hidden):
    hidden[...] = lax.dot_general(
        grad[...], head[...], (((1,), (1,)), ((), ())), preferred_element_type=f32
    ).astype(hidden.dtype)


def params():
    return pltpu.CompilerParams(vmem_limit_bytes=VMEM_LIMIT)


def cost(flops, moved):
    return pl.CostEstimate(flops=flops, bytes_accessed=moved, transcendentals=0)


def logits_call(kernel, meta, pieces, head, extra_in, extra_specs, out_shape, out_specs, scratch):
    depth, width = head.shape
    tile = 256
    anywhere = pl.BlockSpec(memory_space=pl.ANY)
    return pl.pallas_call(
        kernel,
        grid_spec=pltpu.PrefetchScalarGridSpec(
            num_scalar_prefetch=1,
            grid=(width // tile,),
            in_specs=[anywhere] * 8 + [pl.BlockSpec((depth, tile), lambda n, m: (0, n))] + extra_specs,
            out_specs=out_specs,
            scratch_shapes=scratch + [pltpu.SemaphoreType.DMA((32,))],
        ),
        out_shape=out_shape,
        compiler_params=params(),
        cost_estimate=cost(2 * 512 * depth * width, 2 * depth * width + 8 * 512 * 2048),
    )(meta, *pieces, head, *extra_in)


def body(teacher_rows, student_rows, teacher_head, student_head, response_ids, lengths, seq_order):
    depth, width = student_head.shape
    half = depth // 2
    total = response_ids.shape[0]
    own = student_rows.shape[0]
    place = lax.axis_index(AXES)
    c, x, y = place % 2, (place // 8) % SIDE, place // 32

    both = jnp.concatenate([student_rows, teacher_rows], axis=0)
    mine = lax.dynamic_slice_in_dim(both, c * half, half, axis=1)
    theirs = swap(lax.dynamic_slice_in_dim(both, (1 - c) * half, half, axis=1))

    def shard(a, b):
        return jnp.where(c == 0, jnp.concatenate([a, b]), jnp.concatenate([b, a]))

    student_pieces = gather_chips(shard(mine[:own], theirs[:own]))
    teacher_pieces = gather_chips(shard(mine[own:], theirs[own:]))

    position = jnp.arange(4, dtype=jnp.int32)
    inverse = jnp.sum(jnp.where(seq_order[None, :] == position[:, None], position[None, :], 0), axis=1)
    head_meta = jnp.stack([y, x, c, place * width]).astype(jnp.int32)
    student_meta = jnp.concatenate([head_meta, position, lengths])
    teacher_meta = jnp.concatenate([head_meta, inverse, lengths])

    tile = 256
    logits, rows = logits_call(
        student_kernel, student_meta, student_pieces, student_head, [], [],
        [jax.ShapeDtypeStruct((total, width), f32), jax.ShapeDtypeStruct((total, depth), bf16)],
        [pl.BlockSpec((total, tile), lambda n, m: (0, n)), pl.BlockSpec((total, depth), lambda n, m: (0, 0))],
        [],
    )
    fixed = lambda shape: pl.BlockSpec(shape, lambda n, m: (0, 0))
    scaled, spread, stats = logits_call(
        teacher_kernel, teacher_meta, teacher_pieces, teacher_head,
        [logits, response_ids[:, None]], [fixed((total, width)), fixed((total, 1))],
        [
            jax.ShapeDtypeStruct((total, width), f32),
            jax.ShapeDtypeStruct((total, width), f32),
            jax.ShapeDtypeStruct((8, total), f32),
        ],
        [fixed((total, width)), fixed((total, width)), fixed((8, total))],
        [pltpu.VMEM((total, depth), bf16), pltpu.VMEM((total, width), f32), pltpu.VMEM((total, 128), f32)],
    )

    other = swap(stats)
    top_s = jnp.maximum(stats[0], other[0])
    a, b = jnp.exp(stats[0] - top_s), jnp.exp(other[0] - top_s)
    top_t = jnp.maximum(stats[3], other[3])
    chip_t = stats[4] * jnp.exp(stats[3] - top_t) + other[4] * jnp.exp(other[3] - top_t)
    chip_s = jnp.concatenate([top_s, stats[1] * a + other[1] * b, stats[2] * a + other[2] * b])
    chip_t = jnp.stack([top_t, chip_t, stats[5] + other[5]]).reshape(3, CHIPS, 8)
    message = jnp.concatenate(
        [
            jnp.broadcast_to(chip_s[None], (CHIPS, 3 * total)),
            chip_t.transpose(1, 0, 2).reshape(CHIPS, 24),
            jnp.zeros((CHIPS, 104), f32),
        ],
        axis=1,
    )
    gathered = lax.all_to_all(message, AXES, 0, 0, axis_index_groups=CORES, tiled=True)

    block = 512
    count = half // block
    grad, far = pl.pallas_call(
        grad_kernel,
        grid_spec=pltpu.PrefetchScalarGridSpec(
            num_scalar_prefetch=1,
            grid=(count,),
            in_specs=[
                fixed((total, width)),
                fixed((total, width)),
                fixed((8, total)),
                fixed(gathered.shape),
                pl.BlockSpec((block, width), lambda n, m: ((1 - m[2]) * count + n, 0)),
            ],
            out_specs=[fixed((total, width)), pl.BlockSpec((total, block), lambda n, m: (0, n))],
        ),
        out_shape=[
            jax.ShapeDtypeStruct((total, width), bf16),
            jax.ShapeDtypeStruct((total, half), bf16),
        ],
        compiler_params=params(),
        cost_estimate=cost(2 * total * half * width, 12 * total * width + 2 * half * width),
    )(student_meta, scaled, spread, stats, gathered, student_head)
    near = pl.pallas_call(
        hidden_kernel,
        grid_spec=pltpu.PrefetchScalarGridSpec(
            num_scalar_prefetch=1,
            grid=(count,),
            in_specs=[
                fixed((total, width)),
                pl.BlockSpec((block, width), lambda n, m: (m[2] * count + n, 0)),
            ],
            out_specs=pl.BlockSpec((total, block), lambda n, m: (0, n)),
        ),
        out_shape=jax.ShapeDtypeStruct((total, half), f32),
        compiler_params=params(),
        cost_estimate=cost(2 * total * half * width, 4 * total * half + 2 * half * width),
    )(student_meta, grad, student_head)
    chip_sum = (near + swap(far).astype(f32)).astype(bf16)
    parts = lax.all_to_all(chip_sum, AXES, 0, 0, axis_index_groups=CORES, tiled=True)
    head_grad = lax.dot_general(
        rows, grad, (((0,), (0,)), ((), ())), preferred_element_type=f32
    ).astype(bf16)
    mine = jnp.sum(parts.reshape(CHIPS, 8, half).astype(f32), axis=0).astype(bf16)
    keep = lax.dynamic_slice_in_dim(mine, c * own, own)
    take = swap(lax.dynamic_slice_in_dim(mine, (1 - c) * own, own))
    hidden_grad = jnp.where(
        c == 0, jnp.concatenate([keep, take], axis=1), jnp.concatenate([take, keep], axis=1)
    )

    start = place * own
    tokens = lax.dynamic_slice_in_dim(gathered[:, : 3 * total].reshape(CHIPS, 3, total), start, own, axis=2)
    teach = lax.dynamic_slice_in_dim(
        gathered[:, 3 * total : 3 * total + 24].reshape(CHIPS, 3, 8), c * own, own, axis=2
    )
    top = jnp.max(tokens[:, 0], axis=0)
    scale = jnp.exp(tokens[:, 0] - top)
    sums = jnp.sum(tokens[:, 1] * scale, axis=0)
    student_lse = top + jnp.log(sums)
    average = jnp.sum(tokens[:, 2] * scale, axis=0) / sums
    top = jnp.max(teach[:, 0], axis=0)
    teacher_lse = top + jnp.log(jnp.sum(teach[:, 1] * jnp.exp(teach[:, 0] - top), axis=0))
    hit = jnp.sum(teach[:, 2], axis=0)
    span = total // lengths.shape[0]
    index = start + jnp.arange(own, dtype=jnp.int32)
    live = (index % span < lengths[index // span]).astype(f32)
    token_kl = live * (average - student_lse + teacher_lse)
    sampled_gap = live * (hit - student_lse + teacher_lse)
    return (token_kl, sampled_gap, head_grad, hidden_grad)


def solution(mesh):
    in_specs = (P(AXES, None), P(AXES, None), P(None, AXES), P(None, AXES), P(), P(), P())
    out_specs = (P(AXES), P(AXES), P(None, AXES), P(AXES, None))
    return jax.shard_map(body, mesh=mesh, in_specs=in_specs, out_specs=out_specs, check_vma=False)
```

time: 443 us -> 174 us (0.39)
  blocking collectives: 235 us -> 18.9 us
  waiting for transfers between devices: 127 us -> 51.3 us
  Pallas kernels: 0 us -> 37.2 us
  starting transfers between devices: 0.08 us -> 35.6 us
  matrix products: 29.8 us -> 8.59 us
  local copies, waits for them, and re-layouts: 30 us -> 11.5 us
  between operations: 14.1 us -> 0.97 us
  other arithmetic: 4.43 us -> 9.42 us
    psum x2 -> x0, blocking collectives: 173 us -> none  [body(): lax.psum((jnp.sum(scaled, axis=1), jnp.sum(scaled * spread, axis=1), jnp....]
    all_gather x2 -> x0, waiting for transfers between devices: 125 us -> none  [the longest x1 71.7 us: body(): lax.all_gather(student_rows, ('grp', 'voc'), axis=0, tiled=True)]
    pmax x1 -> x0, blocking collectives: 62.4 us -> none  [body(): lax.pmax((jnp.max(student_logits, axis=1), jnp.max(teacher_logits, axis=1...]
    pallas_call x0 -> x4, Pallas kernels: none -> 37.2 us  [the longest x2 23.2 us: logits_call(): pl.pallas_call(kernel, grid_spec=pltpu.PrefetchScalarGridSpec(num_scalar_...]
    all_to_all x0 -> x3, waiting for transfers between devices: none -> 29.9 us  [the longest x1 18 us: body(): lax.all_to_all(chip_sum, AXES, 0, 0, axis_index_groups=CORES, tiled=True)]
    ppermute x0 -> x18, waiting for transfers between devices: none -> 21.5 us  [the longest x6 19.2 us: gather_chips(): lax.ppermute(plane, AXES, along(step))]
    dot_general x4 -> x1, matrix products: 29.8 us -> 8.59 us  [body(): lax.dot_general(rows, grad, (((0,), (0,)), ((), ())), preferred_element_t...]
    ppermute x0 -> x18, starting transfers between devices: none -> 19.4 us  [the longest x12 10.2 us: swap(): return lax.ppermute(value, AXES, SWAP)]
  transfers between devices with their start and end apart: 2 -> 21, of which waited for: 2 -> 10; matrix products, arithmetic and copies ran while one was open for 4% -> 9% of each run, Pallas kernels for 0% -> 9%
where the time goes in v1:
time: 174 us
  waiting for transfers between devices  51.3 us (29%)
  Pallas kernels  37.2 us (21%)
  starting transfers between devices  35.6 us (20%)
  blocking collectives  18.9 us (11%)
  local copies, waits for them, and re-layouts  11.5 us (7%)
  other arithmetic  9.42 us (5%)
  matrix products  8.59 us (5%)
    pallas_call x2, Pallas kernels, logits_call(): pl.pallas_call(kernel, grid_spec=pltpu.PrefetchScalarGridSpec(num_scalar_...  23.2 us
    ppermute x6, waiting for transfers between devices, gather_chips(): lax.ppermute(plane, AXES, along(step))  19.2 us
    all_to_all x1, blocking collectives, body(): lax.all_to_all(message, AXES, 0, 0, axis_index_groups=CORES, tiled=True)  18.9 us
    all_to_all x1, waiting for transfers between devices, body(): lax.all_to_all(chip_sum, AXES, 0, 0, axis_index_groups=CORES, tiled=True)  18 us
    all_to_all x2, waiting for transfers between devices, gather_chips(): lax.all_to_all(wide, AXES, 0, 0, axis_index_groups=PLANES, tiled=True)  11.9 us
    all_to_all x2, starting transfers between devices, gather_chips(): lax.all_to_all(wide, AXES, 0, 0, axis_index_groups=PLANES, tiled=True)  11.4 us
    ppermute x12, starting transfers between devices, swap(): return lax.ppermute(value, AXES, SWAP)  10.2 us
    ppermute x6, starting transfers between devices, gather_chips(): lax.ppermute(plane, AXES, along(step))  9.25 us
  transfers between devices with their start and end apart: 21, of which 10 were waited for; matrix products, arithmetic and copies ran while one was open for 9% of the time, Pallas kernels for 9%

profile of v1, /device:TPU:1, one launch (start us, length us, event | category | flops | bytes accessed | tf_op | source)
XLA Modules:
  0.0 173.5 jit_solution(16827233591694389406)
XLA Ops:
  4.8 7.9 %all-to-all-start.1 = ((bf16[16,8,2048]{2,1,0:T(8,128)(2,1)}), bf16[16,8,2048]{2,1,0:T(8,128)(2,1)S(1)}, u32[]{:S(2)}, u32[]{:S(2)}) async-start(bf16[16,8,2048]{2,1,0:T(8,128)(2,1)} %broadcast_in_dim.25), calls=%async_computation.1 | async-start | bytes 1048576 | tf_op jit(solution)/shard_map/all_to_all | solution.py:46
  12.7 9.9 %all-to-all-done.1 = bf16[16,8,2048]{2,1,0:T(8,128)(2,1)S(1)} async-done(((bf16[16,8,2048]{2,1,0:T(8,128)(2,1)}), bf16[16,8,2048]{2,1,0:T(8,128)(2,1)S(1)}, u32[]{:S(2)}, u32[]{:S(2)}) %all-to-all-start.1) | async-done | bytes 524320 | tf_op jit(solution)/shard_map/all_to_all | solution.py:46
  23.5 3.6 %all-to-all-start = ((bf16[16,8,2048]{2,1,0:T(8,128)(2,1)}), bf16[16,8,2048]{2,1,0:T(8,128)(2,1)S(1)}, u32[]{:S(2)}, u32[]{:S(2)}) async-start(bf16[16,8,2048]{2,1,0:T(8,128)(2,1)} %broadcast_in_dim.24), calls=%async_computation | async-start | bytes 1048576 | tf_op jit(solution)/shard_map/all_to_all | solution.py:46
  27.1 2.8 %collective-permute-start.8 = (bf16[128,2048]{1,0:T(8,128)(2,1)S(1)}, bf16[128,2048]{1,0:T(8,128)(2,1)}, u32[]{:S(2)}, u32[]{:S(2)}) collective-permute-start(bf16[128,2048]{1,0:T(8,128)(2,1)S(1)} %bitcast.54), channel_id=1, source_target_pairs={{0,96},{1,25},{2,98},{3,27},{4,100},{5,29},{6,102},{7,31},{8,104},... | collective-permute-start | bytes 1572872 | tf_op jit(solution)/shard_map/ppermute | solution.py:47
  29.9 1.7 collective-permute-start.10
  31.6 2.4 %collective-permute-start.11 = (bf16[128,2048]{1,0:T(8,128)(2,1)S(1)}, bf16[128,2048]{1,0:T(8,128)(2,1)S(1)}, u32[]{:S(2)}, u32[]{:S(2)}) collective-permute-start(bf16[128,2048]{1,0:T(8,128)(2,1)S(1)} %bitcast.57), channel_id=1, source_target_pairs={{0,1},{1,0},{2,3},{3,2},{4,5},{5,4},{6,7},{7,6},{8,9},{9,8},{10,11... | collective-permute-start | bytes 1572872 | tf_op jit(solution)/shard_map/ppermute | solution.py:41
  34.0 2.0 %all-to-all-done = bf16[16,8,2048]{2,1,0:T(8,128)(2,1)S(1)} async-done(((bf16[16,8,2048]{2,1,0:T(8,128)(2,1)}), bf16[16,8,2048]{2,1,0:T(8,128)(2,1)S(1)}, u32[]{:S(2)}, u32[]{:S(2)}) %all-to-all-start) | async-done | bytes 524320 | tf_op jit(solution)/shard_map/all_to_all | solution.py:46
  36.1 3.5 %collective-permute-start.1 = (bf16[128,2048]{1,0:T(8,128)(2,1)S(1)}, bf16[128,2048]{1,0:T(8,128)(2,1)S(1)}, u32[]{:S(2)}, u32[]{:S(2)}) collective-permute-start(bf16[128,2048]{1,0:T(8,128)(2,1)S(1)} %bitcast.49), channel_id=1, source_target_pairs={{0,96},{1,25},{2,98},{3,27},{4,100},{5,29},{6,102},{7,31},{8,104},... | collective-permute-start | bytes 1572872 | tf_op jit(solution)/shard_map/ppermute | solution.py:47
  39.6 4.5 %collective-permute-done.8.refs_1_ = bf16[128,2048]{1,0:T(8,128)(2,1)} collective-permute-done((bf16[128,2048]{1,0:T(8,128)(2,1)S(1)}, bf16[128,2048]{1,0:T(8,128)(2,1)}, u32[]{:S(2)}, u32[]{:S(2)}) %collective-permute-start.8) | collective-permute-done | bytes 524320 | tf_op jit(solution)/shard_map/ppermute | solution.py:47
  44.1 3.5 %collective-permute-done.9.refs_2_ = bf16[128,2048]{1,0:T(8,128)(2,1)} collective-permute-done((bf16[128,2048]{1,0:T(8,128)(2,1)S(1)}, bf16[128,2048]{1,0:T(8,128)(2,1)}, u32[]{:S(2)}, u32[]{:S(2)}) %collective-permute-start.9) | collective-permute-done | bytes 524320 | tf_op jit(solution)/shard_map/ppermute | solution.py:47
  49.4 5.9 %collective-permute-done.1.refs_1_ = bf16[128,2048]{1,0:T(8,128)(2,1)S(1)} collective-permute-done((bf16[128,2048]{1,0:T(8,128)(2,1)S(1)}, bf16[128,2048]{1,0:T(8,128)(2,1)S(1)}, u32[]{:S(2)}, u32[]{:S(2)}) %collective-permute-start.1) | collective-permute-done | bytes 524320 | tf_op jit(solution)/shard_map/ppermute | solution.py:47
  55.9 5.3 %collective-permute-done.3.refs_3_ = bf16[128,2048]{1,0:T(8,128)(2,1)S(1)} collective-permute-done((bf16[128,2048]{1,0:T(8,128)(2,1)S(1)}, bf16[128,2048]{1,0:T(8,128)(2,1)S(1)}, u32[]{:S(2)}, u32[]{:S(2)}) %collective-permute-start.3) | collective-permute-done | bytes 524320 | tf_op jit(solution)/shard_map/ppermute | solution.py:47
  67.1 1.5 copy.31.refs_10_
  68.6 10.0 %shard_map.102 = (f32[512,768]{1,0:T(8,128)}, bf16[512,4096]{1,0:T(8,128)(2,1)}) custom-call(s32[12]{0:T(128)} %concatenate.56.meta, bf16[128,2048]{1,0:T(8,128)(2,1)} %bitcast.58, bf16[128,2048]{1,0:T(8,128)(2,1)} %collective-permute-done.8.refs_1_, bf16[128,2048]{1,0:T(8,128)(2,1)} %collective-permute-done.9.refs_2_, ...), custom_call_target="tpu_custom_call" | custom-call | flops 3221225472 | bytes 14680064 | tf_op jit(solution)/shard_map/pallas_call | solution.py:180
  79.7 13.2 %shard_map.103 = (f32[512,768]{1,0:T(8,128)}, f32[512,768]{1,0:T(8,128)}, f32[8,512]{1,0:T(8,128)}) custom-call(s32[12]{0:T(128)} %concatenate.52.meta, bf16[128,2048]{1,0:T(8,128)(2,1)} %bitcast.53, bf16[128,2048]{1,0:T(8,128)(2,1)} %copy-done.3, bf16[128,2048]{1,0:T(8,128)(2,1)} %copy-done.4, bf16[128,2048]{1,0:T(8,128)(2,1)} %copy-done.5, ...), custom_call_target="tpu_custom_call" | custom-call | flops 3221225472 | bytes 14680064 | tf_op jit(solution)/shard_map/pallas_call | solution.py:180
  96.5 18.9 %all_to_all.36 = f32[64,1,1664]{2,1,0:T(1,128)S(1)} all-to-all(f32[64,1,1664]{2,1,0:T(1,128)S(1)} %all_to_all.27), channel_id=1, replica_groups={{0,2,4,6,8,10,12,14,16,18,20,22,24,26,28,30,32,34,36,38,40,42,44,46,48,..., dimensions={0} | all-to-all | bytes 851968 | tf_op jit(solution)/shard_map/all_to_all | solution.py:254
  116.2 7.5 %shard_map.104 = (bf16[512,768]{1,0:T(8,128)(2,1)}, bf16[512,2048]{1,0:T(8,128)(2,1)}) custom-call(s32[12]{0:T(128)} %concatenate.56.meta, f32[512,768]{1,0:T(8,128)} %get-tuple-element.14.scaled, f32[512,768]{1,0:T(8,128)} %get-tuple-element.15.spread, f32[8,512]{1,0:T(8,128)} %get-tuple-element.12.stats, f32[64,1664]{1,0:T(8,128)} %bitcast.46, ...), custom_call_target="tpu_custom_call" | custom-call | flops 1610612736 | bytes 7864320 | tf_op jit(solution)/shard_map/pallas_call | solution.py:258
  123.8 1.9 %collective-permute-start.16 = (bf16[512,2048]{1,0:T(8,128)(2,1)}, bf16[512,2048]{1,0:T(8,128)(2,1)S(1)}, u32[]{:S(2)}, u32[]{:S(2)}) collective-permute-start(bf16[512,2048]{1,0:T(8,128)(2,1)} %get-tuple-element.17), channel_id=1, source_target_pairs={{0,1},{1,0},{2,3},{3,2},{4,5},{5,4},{6,7},{7,6},{8,9},{9,8},{10,11... | collective-permute-start | bytes 6291464 | tf_op jit(solution)/shard_map/ppermute | solution.py:41
  125.7 6.4 %shard_map.105 = f32[512,2048]{1,0:T(8,128)} custom-call(s32[12]{0:T(128)} %concatenate.56.meta, bf16[512,768]{1,0:T(8,128)(2,1)} %get-tuple-element.16.grad, bf16[4096,768]{1,0:T(8,128)(2,1)} %head.3), custom_call_target="tpu_custom_call" | custom-call | flops 1610612736 | bytes 7340032 | tf_op jit(solution)/shard_map/pallas_call | solution.py:279
  132.1 4.3 %fusion = bf16[64,8,2048]{2,1,0:T(8,128)(2,1)} fusion(f32[512,2048]{1,0:T(8,128)} %shard_map.105, bf16[512,2048]{1,0:T(8,128)(2,1)S(1)} %collective-permute-done.16), kind=kLoop, calls=%fused_computation.3 | loop fusion | flops 3145728 | bytes 8388608 | tf_op jit(solution)/shard_map/all_to_all | solution.py:295
  136.4 4.8 %all-to-all-start.3 = ((bf16[64,8,2048]{2,1,0:T(8,128)(2,1)}), bf16[64,8,2048]{2,1,0:T(8,128)(2,1)S(1)}, u32[]{:S(2)}, u32[]{:S(2)}) async-start(bf16[64,8,2048]{2,1,0:T(8,128)(2,1)} %fusion), calls=%async_computation.3 | async-start | bytes 4194304 | tf_op jit(solution)/shard_map/all_to_all | solution.py:295
  143.5 8.6 %convolution_convert_fusion = bf16[4096,768]{1,0:T(8,128)(2,1)} fusion(bf16[512,4096]{1,0:T(8,128)(2,1)} %get-tuple-element.13, bf16[512,768]{1,0:T(8,128)(2,1)} %get-tuple-element.16.grad), kind=kOutput, calls=%fused_computation.1 | convolution fusion | flops 3224371200 | bytes 11272192 | tf_op jit(solution)/shard_map/dot_general | solution.py:296
  152.1 18.0 %all-to-all-done.3 = bf16[64,8,2048]{2,1,0:T(8,128)(2,1)S(1)} async-done(((bf16[64,8,2048]{2,1,0:T(8,128)(2,1)}), bf16[64,8,2048]{2,1,0:T(8,128)(2,1)S(1)}, u32[]{:S(2)}, u32[]{:S(2)}) %all-to-all-start.3) | async-done | bytes 2097184 | tf_op jit(solution)/shard_map/all_to_all | solution.py:295
  170.4 1.6 collective-permute-start.17
  (95 shorter events, 22.7 us)
Async XLA Ops:
  1.5 2.4 %collective-permute-start = (bf16[8,2048]{1,0:T(8,128)(2,1)S(1)}, bf16[8,2048]{1,0:T(8,128)(2,1)S(1)}, u32[]{:S(2)}, u32[]{:S(2)}) collective-permute-start(bf16[8,2048]{1,0:T(8,128)(2,1)S(1)} %get-tuple-element.33), channel_id=1, source_target_pairs={{0,1},{1,0},{2,3},{3,2},{4,5},{5,4},{6,7},{7,6},{8,9},{9,8},{10,11... | collective-permute-start | bytes 98312 | tf_op jit(solution)/shard_map/ppermute | solution.py:41
  4.8 17.8 %all-to-all-start.1 = ((bf16[16,8,2048]{2,1,0:T(8,128)(2,1)}), bf16[16,8,2048]{2,1,0:T(8,128)(2,1)S(1)}, u32[]{:S(2)}, u32[]{:S(2)}) async-start(bf16[16,8,2048]{2,1,0:T(8,128)(2,1)} %broadcast_in_dim.25), calls=%async_computation.1 | async-start | bytes 1048576 | tf_op jit(solution)/shard_map/all_to_all | solution.py:46
  22.6 32.9 %copy-start.8 = (bf16[16,8,2048]{2,1,0:T(8,128)(2,1)}, bf16[16,8,2048]{2,1,0:T(8,128)(2,1)S(1)}, u32[]{:S(2)}) copy-start(bf16[16,8,2048]{2,1,0:T(8,128)(2,1)S(1)} %all-to-all-done.1) | copy-start | bytes 1572868
  23.5 12.5 %all-to-all-start = ((bf16[16,8,2048]{2,1,0:T(8,128)(2,1)}), bf16[16,8,2048]{2,1,0:T(8,128)(2,1)S(1)}, u32[]{:S(2)}, u32[]{:S(2)}) async-start(bf16[16,8,2048]{2,1,0:T(8,128)(2,1)} %broadcast_in_dim.24), calls=%async_computation | async-start | bytes 1048576 | tf_op jit(solution)/shard_map/all_to_all | solution.py:46
  27.1 17.0 %collective-permute-start.8 = (bf16[128,2048]{1,0:T(8,128)(2,1)S(1)}, bf16[128,2048]{1,0:T(8,128)(2,1)}, u32[]{:S(2)}, u32[]{:S(2)}) collective-permute-start(bf16[128,2048]{1,0:T(8,128)(2,1)S(1)} %bitcast.54), channel_id=1, source_target_pairs={{0,96},{1,25},{2,98},{3,27},{4,100},{5,29},{6,102},{7,31},{8,104},... | collective-permute-start | bytes 1572872 | tf_op jit(solution)/shard_map/ppermute | solution.py:47
  29.9 17.7 %collective-permute-start.9 = (bf16[128,2048]{1,0:T(8,128)(2,1)S(1)}, bf16[128,2048]{1,0:T(8,128)(2,1)}, u32[]{:S(2)}, u32[]{:S(2)}) collective-permute-start(bf16[128,2048]{1,0:T(8,128)(2,1)S(1)} %bitcast.55), channel_id=1, source_target_pairs={{0,32},{1,9},{2,34},{3,11},{4,36},{5,13},{6,38},{7,15},{8,40},{9,1... | collective-permute-start | bytes 1572872 | tf_op jit(solution)/shard_map/ppermute | solution.py:47
  29.9 18.9 %collective-permute-start.10 = (bf16[128,2048]{1,0:T(8,128)(2,1)S(1)}, bf16[128,2048]{1,0:T(8,128)(2,1)}, u32[]{:S(2)}, u32[]{:S(2)}) collective-permute-start(bf16[128,2048]{1,0:T(8,128)(2,1)S(1)} %bitcast.56), channel_id=1, source_target_pairs={{0,64},{1,17},{2,66},{3,19},{4,68},{5,21},{6,70},{7,23},{8,72},{9,... | collective-permute-start | bytes 1572872 | tf_op jit(solution)/shard_map/ppermute | solution.py:47
  31.6 17.7 %collective-permute-start.11 = (bf16[128,2048]{1,0:T(8,128)(2,1)S(1)}, bf16[128,2048]{1,0:T(8,128)(2,1)S(1)}, u32[]{:S(2)}, u32[]{:S(2)}) collective-permute-start(bf16[128,2048]{1,0:T(8,128)(2,1)S(1)} %bitcast.57), channel_id=1, source_target_pairs={{0,1},{1,0},{2,3},{3,2},{4,5},{5,4},{6,7},{7,6},{8,9},{9,8},{10,11... | collective-permute-start | bytes 1572872 | tf_op jit(solution)/shard_map/ppermute | solution.py:41
  36.1 42.6 %copy-start.2 = (bf16[16,8,2048]{2,1,0:T(8,128)(2,1)}, bf16[16,8,2048]{2,1,0:T(8,128)(2,1)S(1)}, u32[]{:S(2)}) copy-start(bf16[16,8,2048]{2,1,0:T(8,128)(2,1)S(1)} %all-to-all-done) | copy-start | bytes 1572868
  36.1 19.2 %collective-permute-start.1 = (bf16[128,2048]{1,0:T(8,128)(2,1)S(1)}, bf16[128,2048]{1,0:T(8,128)(2,1)S(1)}, u32[]{:S(2)}, u32[]{:S(2)}) collective-permute-start(bf16[128,2048]{1,0:T(8,128)(2,1)S(1)} %bitcast.49), channel_id=1, source_target_pairs={{0,96},{1,25},{2,98},{3,27},{4,100},{5,29},{6,102},{7,31},{8,104},... | collective-permute-start | bytes 1572872 | tf_op jit(solution)/shard_map/ppermute | solution.py:47
  44.1 11.4 %collective-permute-start.2 = (bf16[128,2048]{1,0:T(8,128)(2,1)S(1)}, bf16[128,2048]{1,0:T(8,128)(2,1)S(1)}, u32[]{:S(2)}, u32[]{:S(2)}) collective-permute-start(bf16[128,2048]{1,0:T(8,128)(2,1)S(1)} %bitcast.50), channel_id=1, source_target_pairs={{0,32},{1,9},{2,34},{3,11},{4,36},{5,13},{6,38},{7,15},{8,40},{9,1... | collective-permute-start | bytes 1572872 | tf_op jit(solution)/shard_map/ppermute | solution.py:47
  47.6 13.7 %collective-permute-start.3 = (bf16[128,2048]{1,0:T(8,128)(2,1)S(1)}, bf16[128,2048]{1,0:T(8,128)(2,1)S(1)}, u32[]{:S(2)}, u32[]{:S(2)}) collective-permute-start(bf16[128,2048]{1,0:T(8,128)(2,1)S(1)} %bitcast.51), channel_id=1, source_target_pairs={{0,64},{1,17},{2,66},{3,19},{4,68},{5,21},{6,70},{7,23},{8,72},{9,... | collective-permute-start | bytes 1572872 | tf_op jit(solution)/shard_map/ppermute | solution.py:47
  48.8 13.3 %collective-permute-start.12 = (bf16[128,2048]{1,0:T(8,128)(2,1)}, bf16[128,2048]{1,0:T(8,128)(2,1)S(1)}, u32[]{:S(2)}, u32[]{:S(2)}) collective-permute-start(bf16[128,2048]{1,0:T(8,128)(2,1)} %collective-permute-done.8.refs_1_), channel_id=1, source_target_pairs={{0,1},{1,0},{2,3},{3,2},{4,5},{5,4},{6,7},{7,6},{8,9},{9,8},{10,11... | collective-permute-start | bytes 1572872 | tf_op jit(solution)/shard_map/ppermute | solution.py:41
  49.3 13.6 %collective-permute-start.13 = (bf16[128,2048]{1,0:T(8,128)(2,1)}, bf16[128,2048]{1,0:T(8,128)(2,1)S(1)}, u32[]{:S(2)}, u32[]{:S(2)}) collective-permute-start(bf16[128,2048]{1,0:T(8,128)(2,1)} %collective-permute-done.9.refs_2_), channel_id=1, source_target_pairs={{0,1},{1,0},{2,3},{3,2},{4,5},{5,4},{6,7},{7,6},{8,9},{9,8},{10,11... | collective-permute-start | bytes 1572872 | tf_op jit(solution)/shard_map/ppermute | solution.py:41
  55.3 23.4 %copy-start.3 = (bf16[128,2048]{1,0:T(8,128)(2,1)}, bf16[128,2048]{1,0:T(8,128)(2,1)S(1)}, u32[]{:S(2)}) copy-start(bf16[128,2048]{1,0:T(8,128)(2,1)S(1)} %collective-permute-done.1.refs_1_) | copy-start | bytes 1572868
  55.3 13.3 %collective-permute-start.14 = (bf16[128,2048]{1,0:T(8,128)(2,1)}, bf16[128,2048]{1,0:T(8,128)(2,1)}, u32[]{:S(2)}, u32[]{:S(2)}) collective-permute-start(bf16[128,2048]{1,0:T(8,128)(2,1)} %collective-permute-done.10.refs_3_), channel_id=1, source_target_pairs={{0,1},{1,0},{2,3},{3,2},{4,5},{5,4},{6,7},{7,6},{8,9},{9,8},{10,11... | collective-permute-start | bytes 1572872 | tf_op jit(solution)/shard_map/ppermute | solution.py:41
  55.5 23.3 %collective-permute-start.4 = (bf16[128,2048]{1,0:T(8,128)(2,1)S(1)}, bf16[128,2048]{1,0:T(8,128)(2,1)S(1)}, u32[]{:S(2)}, u32[]{:S(2)}) collective-permute-start(bf16[128,2048]{1,0:T(8,128)(2,1)S(1)} %bitcast.52), channel_id=1, source_target_pairs={{0,1},{1,0},{2,3},{3,2},{4,5},{5,4},{6,7},{7,6},{8,9},{9,8},{10,11... | collective-permute-start | bytes 1572872 | tf_op jit(solution)/shard_map/ppermute | solution.py:41
  61.2 17.5 %collective-permute-start.5 = (bf16[128,2048]{1,0:T(8,128)(2,1)S(1)}, bf16[128,2048]{1,0:T(8,128)(2,1)S(1)}, u32[]{:S(2)}, u32[]{:S(2)}) collective-permute-start(bf16[128,2048]{1,0:T(8,128)(2,1)S(1)} %collective-permute-done.1.refs_1_), channel_id=1, source_target_pairs={{0,1},{1,0},{2,3},{3,2},{4,5},{5,4},{6,7},{7,6},{8,9},{9,8},{10,11... | collective-permute-start | bytes 1572872 | tf_op jit(solution)/shard_map/ppermute | solution.py:41
  62.1 16.7 %collective-permute-start.6 = (bf16[128,2048]{1,0:T(8,128)(2,1)S(1)}, bf16[128,2048]{1,0:T(8,128)(2,1)}, u32[]{:S(2)}, u32[]{:S(2)}) collective-permute-start(bf16[128,2048]{1,0:T(8,128)(2,1)S(1)} %collective-permute-done.2.refs_2_), channel_id=1, source_target_pairs={{0,1},{1,0},{2,3},{3,2},{4,5},{5,4},{6,7},{7,6},{8,9},{9,8},{10,11... | collective-permute-start | bytes 1572872 | tf_op jit(solution)/shard_map/ppermute | solution.py:41
  63.6 15.1 %collective-permute-start.7 = (bf16[128,2048]{1,0:T(8,128)(2,1)S(1)}, bf16[128,2048]{1,0:T(8,128)(2,1)}, u32[]{:S(2)}, u32[]{:S(2)}) collective-permute-start(bf16[128,2048]{1,0:T(8,128)(2,1)S(1)} %collective-permute-done.3.refs_3_), channel_id=1, source_target_pairs={{0,1},{1,0},{2,3},{3,2},{4,5},{5,4},{6,7},{7,6},{8,9},{9,8},{10,11... | collective-permute-start | bytes 1572872 | tf_op jit(solution)/shard_map/ppermute | solution.py:41
  92.9 1.6 collective-permute-start.15
  123.8 8.3 %collective-permute-start.16 = (bf16[512,2048]{1,0:T(8,128)(2,1)}, bf16[512,2048]{1,0:T(8,128)(2,1)S(1)}, u32[]{:S(2)}, u32[]{:S(2)}) collective-permute-start(bf16[512,2048]{1,0:T(8,128)(2,1)} %get-tuple-element.17), channel_id=1, source_target_pairs={{0,1},{1,0},{2,3},{3,2},{4,5},{5,4},{6,7},{7,6},{8,9},{9,8},{10,11... | collective-permute-start | bytes 6291464 | tf_op jit(solution)/shard_map/ppermute | solution.py:41
  136.4 33.7 %all-to-all-start.3 = ((bf16[64,8,2048]{2,1,0:T(8,128)(2,1)}), bf16[64,8,2048]{2,1,0:T(8,128)(2,1)S(1)}, u32[]{:S(2)}, u32[]{:S(2)}) async-start(bf16[64,8,2048]{2,1,0:T(8,128)(2,1)} %fusion), calls=%async_computation.3 | async-start | bytes 4194304 | tf_op jit(solution)/shard_map/all_to_all | solution.py:295
  170.4 2.5 %collective-permute-start.17 = (bf16[4,2048]{1,0:T(4,128)(2,1)S(1)}, bf16[4,2048]{1,0:T(4,128)(2,1)S(1)}, u32[]{:S(2)}, u32[]{:S(2)}) collective-permute-start(bf16[4,2048]{1,0:T(4,128)(2,1)S(1)} %get-tuple-element.35), channel_id=1, source_target_pairs={{0,1},{1,0},{2,3},{3,2},{4,5},{5,4},{6,7},{7,6},{8,9},{9,8},{10,11... | collective-permute-start | bytes 49160 | tf_op jit(solution)/shard_map/ppermute | solution.py:41
  (9 other events, 61.1 us)
